TPU v7x, 256 devices: a whole 4x4x8 slice. The times are simulated.
256 devices in a mesh: context: 32 (over x, z), mp: 8 (over y, core).
Axes of the slice: x: 4, y: 4, z: 8, core: 2. Of those that a mesh axis runs over, the one named last changes fastest.
Arguments:
- queries: bfloat16 [4096, 8192], P('context', 'mp'), may hold values from -12 to 12
- query_pos: int32 [4096], P('context'), may hold values from 0 to 131071, as said below
- k_cache: bfloat16 [131072, 1024], P('context', 'mp'), may hold values from -6 to 6
- v_cache: bfloat16 [131072, 1024], P('context', 'mp'), may hold values from -6 to 6
- kept_index: int32 [16384], P('context'), may hold values from 0 to 4095, as said below
- kept_count: int32 [32], P('context'), may hold values from 1 to 512, as said below
- route: int32 [4096], P('context'), may hold values from 0 to 4095, as said below
Outputs:
- balanced_out: bfloat16 [4096, 8192], P('context', 'mp')
Inputs may be any that keep to these rules, and one draw needn't show every extreme that they name: `query_pos`: each context index's 128 entries lie in its own block of 4096 positions, distinct and ascending. `kept_index`: each context index's 512 entries are local positions in its block; the live ones come first, distinct and ascending, and the rest are 0. The list of context index 0 starts with position 0. `kept_count`: some context index has all 512 slots live. `route`: A permutation of the 4096 rows; the rows of one context index go in equal shares to the blocks of 128 output rows of all context indices.
All inputs are finite; a program needn't handle non-finite values.
Results may differ from a plain program's by a relative error of at most 0.018.
Values may be sent and summed in bfloat16 or wider, within the bound.
A program may use at most 128 MiB of HBM per device.

v0:
```python
import math

import jax
import jax.numpy as jnp
from jax import lax
from jax.sharding import PartitionSpec as P

HD = 128


far_away = 2**30
neg_large = -1e30


def span_of(row_total, most):
    span_rows = row_total
    while span_rows > most and span_rows % 2 == 0:
        span_rows = span_rows // 2
    return span_rows


def kept_local(k_cache, v_cache, kept_index, kept_count):
    local_rows = k_cache.shape[0]
    device_index = lax.axis_index("context")
    slot_ids = jnp.arange(kept_index.shape[0], dtype=jnp.int32)
    kept_keys = jnp.take(k_cache, kept_index, axis=0)
    kept_vals = jnp.take(v_cache, kept_index, axis=0)
    key_pos = jnp.where(slot_ids < kept_count[0], kept_index + device_index * local_rows, far_away)
    return (kept_keys, kept_vals, key_pos)


def scores_of(query_block, key_tile, kv_heads):
    row_total = query_block.shape[0]
    head_count = query_block.shape[1] // HD
    group_size = head_count // kv_heads
    query_heads = query_block.reshape(row_total, kv_heads, group_size, HD)
    key_heads = key_tile.reshape(key_tile.shape[0], kv_heads, HD)
    scores = jnp.einsum(
        "qhgd,khd->qhgk", query_heads, key_heads, preferred_element_type=jnp.float32
    )
    return scores.reshape(row_total, head_count, key_tile.shape[0]) * (1.0 / math.sqrt(HD))


def weigh_values(weights_bf, value_tile, kv_heads):
    row_total, head_count, tile_rows = weights_bf.shape
    group_size = head_count // kv_heads
    value_heads = value_tile.reshape(tile_rows, kv_heads, HD)
    summed = jnp.einsum(
        "qhgk,khd->qhgd",
        weights_bf.reshape(row_total, kv_heads, group_size, tile_rows),
        value_heads,
        preferred_element_type=jnp.float32,
    )
    return summed.reshape(row_total, head_count, HD)


def block_update(state, query_block, pos_block, key_tile, value_tile, pos_tile, kv_heads):
    row_peak, denominator, numerator = state
    scores = scores_of(query_block, key_tile, kv_heads)
    visible = pos_tile[None, None, :] <= pos_block[:, None, None]
    scores = jnp.where(visible, scores, neg_large)
    new_peak = jnp.maximum(row_peak, jnp.max(scores, axis=-1))
    weights = jnp.where(visible, jnp.exp(scores - new_peak[..., None]), 0.0)
    rescale = jnp.exp(row_peak - new_peak)
    denominator = denominator * rescale + jnp.sum(weights, axis=-1)
    numerator = numerator * rescale[..., None] + weigh_values(
        weights.astype(jnp.bfloat16), value_tile, kv_heads
    )
    return (new_peak, denominator, numerator)


def attend(queries, query_pos, kept_keys, kept_vals, key_pos):
    row_total = queries.shape[0]
    head_count = queries.shape[1] // HD
    kv_heads = kept_keys.shape[1] // HD
    block_rows = span_of(row_total, 64)
    initial = (
        jnp.full((row_total, head_count), neg_large, jnp.float32),
        jnp.zeros((row_total, head_count), jnp.float32),
        jnp.zeros((row_total, head_count, HD), jnp.float32),
    )
    key_piece = lax.all_gather(kept_keys, "context", axis=0, tiled=True)
    value_piece = lax.all_gather(kept_vals, "context", axis=0, tiled=True)
    pos_piece = lax.all_gather(key_pos, "context", axis=0, tiled=True)
    tile_rows = span_of(key_piece.shape[0], 1536)
    tile_count = key_piece.shape[0] // tile_rows

    def tile_step(step_index, state):
        key_tile = lax.dynamic_slice_in_dim(key_piece, step_index * tile_rows, tile_rows, 0)
        value_tile = lax.dynamic_slice_in_dim(value_piece, step_index * tile_rows, tile_rows, 0)
        pos_tile = lax.dynamic_slice_in_dim(pos_piece, step_index * tile_rows, tile_rows, 0)
        pieces_out = []
        for block in range(row_total // block_rows):
            lower = block * block_rows
            upper = lower + block_rows
            block_state = tuple((member[lower:upper] for member in state))
            query_block = queries[lower:upper]
            pos_block = query_pos[lower:upper]
            skipped = jnp.min(pos_tile) > jnp.max(pos_block)
            block_state = lax.cond(
                skipped,
                lambda state_in: state_in,
                lambda state_in: block_update(
                    state_in, query_block, pos_block, key_tile, value_tile, pos_tile, kv_heads
                ),
                block_state,
            )
            pieces_out.append(block_state)
        return tuple(
            (jnp.concatenate([member[index] for member in pieces_out], 0) for index in range(3))
        )

    row_peak, denominator, numerator = lax.fori_loop(0, tile_count, tile_step, initial)
    return (
        (numerator / denominator[..., None])
        .reshape(row_total, head_count * HD)
        .astype(jnp.bfloat16)
    )


def per_device(queries, query_pos, k_cache, v_cache, kept_index, kept_count, route):
    kept_keys, kept_vals, key_pos = kept_local(k_cache, v_cache, kept_index, kept_count)
    row_total = queries.shape[0]
    device_index = lax.axis_index("context")
    destination = route // row_total
    send_order = jnp.argsort(destination, stable=True)
    attended = attend(queries, query_pos, kept_keys, kept_vals, key_pos)
    result, routes_in = (
        lax.all_to_all(attended[send_order], "context", split_axis=0, concat_axis=0, tiled=True),
        lax.all_to_all(route[send_order], "context", split_axis=0, concat_axis=0, tiled=True),
    )
    slot_ids = routes_in - device_index * row_total
    balanced_out = jnp.zeros_like(result).at[slot_ids].set(result)
    return balanced_out


def solution(mesh):
    placed = (
        P("context", "mp"),
        P("context"),
        P("context", "mp"),
        P("context", "mp"),
        P("context"),
        P("context"),
        P("context"),
    )
    return jax.shard_map(
        per_device, mesh=mesh, in_specs=placed, out_specs=P("context", "mp"), check_vma=False
    )
```

profile of v0, /device:TPU:20, one launch (start us, length us, event | category | flops | bytes accessed | tf_op | source)
XLA Modules:
  0.0 348.0 jit_solution(8593066953242271571)
XLA Ops:
  8.7 1.3 gather_fusion.2
  10.0 2.4 gather_fusion.3
  12.5 0.8 broadcast_select_fusion
  14.1 2.6 sort.17
  16.7 1.2 gather_fusion
  18.7 11.6 %all-to-all-start = ((s32[32,4,1]{1,2,0:T(1,128)}), s32[32,4,1]{1,2,0:T(1,128)S(1)}, u32[]{:S(2)}, u32[]{:S(2)}) async-start(s32[32,4,1]{1,2,0:T(1,128)} %bitcast.14), calls=%async_computation | async-start | bytes 32768 | tf_op jit(solution)/shard_map/all_to_all | solution.py:130
  30.3 48.2 %all-gather = s32[32,1,512]{2,1,0:T(1,128)S(1)} all-gather(s32[1,1,512]{2,1,0:T(1,128)S(1)} %bitcast.99), channel_id=1, replica_groups=mesh['context'=32,'mp'=8] {'context'}, dimensions={0}, use_global_device_ids=true | all-gather | bytes 67584 | tf_op jit(solution)/shard_map/all_gather | solution.py:84
  79.2 17.3 %all-gather.4.cloned.1.call-done = bf16[16384,128]{1,0:T(8,128)(2,1)} async-done(((bf16[512,128]{1,0:T(8,128)(2,1)}), bf16[16384,128]{1,0:T(8,128)(2,1)}) %all-gather.4.cloned.1.call-update) | async-done | bytes 4194320 | tf_op jit(solution)/shard_map/all_gather | solution.py:82
  96.5 81.7 %all-gather.6.cloned.1.call-done = bf16[16384,128]{1,0:T(8,128)(2,1)} async-done(((bf16[512,128]{1,0:T(8,128)(2,1)}), bf16[16384,128]{1,0:T(8,128)(2,1)}) %all-gather.6.cloned.1.call-update) | async-done | bytes 4194320 | tf_op jit(solution)/shard_map/all_gather | solution.py:83
  178.2 113.5 %while.18 = (s32[]{:T(128)}, f32[128,8]{0,1:T(8,128)S(1)}, f32[128,8]{0,1:T(8,128)S(1)}, f32[128,8,128]{2,0,1:T(8,128)S(1)}, s32[16384]{0:T(1024)S(1)}, /*index=...) while((s32[]{:T(128)}, f32[128,8]{0,1:T(8,128)S(1)}, ...), condition=%wide.region_13.15_spmd, body=%wide.region_3.14_spmd.sunk | while | flops 551031808 | bytes 18720196 | solution.py:113
  178.3 1.1 constant_dynamic-slice_fusion.3
  181.4 2.1 conditional.5
  184.8 2.2 conditional.4
  187.2 1.1 constant_dynamic-slice_fusion.3
  190.4 2.1 conditional.5
  193.8 2.2 conditional.4
  196.2 1.1 constant_dynamic-slice_fusion.3
  199.4 2.1 conditional.5
  202.8 2.2 conditional.4
  205.2 1.1 constant_dynamic-slice_fusion.3
  208.3 2.1 conditional.5
  211.7 2.2 conditional.4
  214.1 1.1 constant_dynamic-slice_fusion.3
  217.3 2.1 conditional.5
  220.7 2.2 conditional.4
  223.1 1.1 constant_dynamic-slice_fusion.3
  226.3 2.1 conditional.5
  229.7 2.2 conditional.4
  232.1 1.1 constant_dynamic-slice_fusion.3
  235.2 2.1 conditional.5
  238.7 2.2 conditional.4
  241.1 1.1 constant_dynamic-slice_fusion.3
  244.2 2.1 conditional.5
  247.6 2.2 conditional.4
  250.0 1.1 constant_dynamic-slice_fusion.3
  253.2 2.1 conditional.5
  256.6 2.2 conditional.4
  259.0 1.1 constant_dynamic-slice_fusion.3
  263.7 1.1 constant_dynamic-slice_fusion.3
  268.4 1.1 constant_dynamic-slice_fusion.3
  273.1 1.1 constant_dynamic-slice_fusion.3
  277.7 1.1 constant_dynamic-slice_fusion.3
  282.4 1.1 constant_dynamic-slice_fusion.3
  287.1 1.1 constant_dynamic-slice_fusion.3
  292.0 0.9 gather_fusion.1
  293.7 36.5 %all-to-all-start.1 = ((bf16[32,4,1024]{2,1,0:T(4,128)(2,1)}), bf16[32,4,1024]{2,1,0:T(4,128)(2,1)S(1)}, u32[]{:S(2)}, u32[]{:S(2)}) async-start(bf16[32,4,1024]{2,1,0:T(4,128)(2,1)} %all_to_all.16), calls=%async_computation.1 | async-start | bytes 524288 | tf_op jit(solution)/shard_map/all_to_all | solution.py:129
  330.3 9.0 %all-to-all-done.1 = bf16[32,4,1024]{2,1,0:T(4,128)(2,1)S(1)} async-done(((bf16[32,4,1024]{2,1,0:T(4,128)(2,1)}), bf16[32,4,1024]{2,1,0:T(4,128)(2,1)S(1)}, u32[]{:S(2)}, u32[]{:S(2)}) %all-to-all-start.1) | async-done | bytes 262176 | tf_op jit(solution)/shard_map/all_to_all | solution.py:129
  339.4 1.8 scatter_custom_fusion
  (272 shorter events, 58.3 us)
Async XLA Ops:
  6.5 2.1 copy-start
  6.5 7.5 %copy-start.1 = (s32[128]{0:T(128)S(1)}, s32[128]{0:T(128)}, u32[]{:S(2)}) copy-start(s32[128]{0:T(128)} %param.21) | copy-start | bytes 1540
  6.5 71.9 %copy-start.3 = (s32[128]{0:T(128)S(1)}, s32[128]{0:T(128)}, u32[]{:S(2)}) copy-start(s32[128]{0:T(128)} %param.16) | copy-start | bytes 1540
  6.5 90.0 %all-gather.4.cloned.1.call-start = ((), (), s32[]{:S(2)}) async-start(), calls=%async_computation.2 | async-start | bytes 4325376 | tf_op jit(solution)/shard_map/all_gather | solution.py:82
  8.7 169.6 %copy-start.2 = (bf16[128,1024]{1,0:T(8,128)(2,1)S(1)}, bf16[128,1024]{1,0:T(8,128)(2,1)}, u32[]{:S(2)}) copy-start(bf16[128,1024]{1,0:T(8,128)(2,1)} %param.15) | copy-start | bytes 786436
  13.3 164.9 %all-gather.6.cloned.1.call-start = ((), (), s32[]{:S(2)}) async-start(), calls=%async_computation.3 | async-start | bytes 4325376 | tf_op jit(solution)/shard_map/all_gather | solution.py:83
  18.7 275.0 %all-to-all-start = ((s32[32,4,1]{1,2,0:T(1,128)}), s32[32,4,1]{1,2,0:T(1,128)S(1)}, u32[]{:S(2)}, u32[]{:S(2)}) async-start(s32[32,4,1]{1,2,0:T(1,128)} %bitcast.14), calls=%async_computation | async-start | bytes 32768 | tf_op jit(solution)/shard_map/all_to_all | solution.py:130
  293.7 45.6 %all-to-all-start.1 = ((bf16[32,4,1024]{2,1,0:T(4,128)(2,1)}), bf16[32,4,1024]{2,1,0:T(4,128)(2,1)S(1)}, u32[]{:S(2)}, u32[]{:S(2)}) async-start(bf16[32,4,1024]{2,1,0:T(4,128)(2,1)} %all_to_all.16), calls=%async_computation.1 | async-start | bytes 524288 | tf_op jit(solution)/shard_map/all_to_all | solution.py:129
Sparse Core Ops, SparseCore 0:
  13.4 83.0 all-gather.3
  99.1 79.0 all-gather.5
where the time goes:
time: 351 us; the launch traced here: 348 us
  waiting for transfers between devices  109 us (31%)
  blocking collectives  48.2 us (14%)
  starting transfers between devices  48.1 us (14%)
  loops' own time  43.4 us (12%)
  other arithmetic  33.6 us (10%)
  local copies, waits for them, and re-layouts  28.8 us (8%)
  matrix products  22.9 us (7%)
  between operations  14.3 us (4%)
    all_gather x1, waiting for transfers between devices, attend(): value_piece = lax.all_gather(kept_vals, 'context', axis=0, tiled=True)  81.7 us
    all_gather x1, blocking collectives, attend(): pos_piece = lax.all_gather(key_pos, 'context', axis=0, tiled=True)  48.2 us
    another operation x1, loops' own time, attend(): lax.fori_loop(0, tile_count, tile_step, initial)  42.3 us
    all_to_all x1, starting transfers between devices, per_device(): lax.all_to_all(attended[send_order], 'context', split_axis=0, concat_axis...  36.5 us
    all_gather x1, waiting for transfers between devices, attend(): key_piece = lax.all_gather(kept_keys, 'context', axis=0, tiled=True)  17.3 us
    dynamic_slice x16, local copies, waits for them, and re-layouts, tile_step(): lax.dynamic_slice_in_dim(value_piece, step_index * tile_rows, tile_rows, 0)  17 us
    dot_general x18, matrix products, weigh_values(): jnp.einsum('qhgk,khd->qhgd', weights_bf.reshape(row_total, kv_heads, grou...  12.8 us
    reduce_sum x18, other arithmetic, block_update(): denominator = denominator * rescale + jnp.sum(weights, axis=-1)  12.4 us
  transfers between devices with their start and end apart: 4, of which 3 were waited for; matrix products, arithmetic and copies ran while one was open for 22% of the time, Pallas kernels for 0%

commit v1 on v0

v1 whole, which is shorter than its diff:
```python
import math

import jax
import jax.numpy as jnp
from jax import lax
from jax.experimental import pallas as pl
from jax.experimental.pallas import tpu as pltpu
from jax.sharding import PartitionSpec as P

MESH = pl.DeviceIdType.MESH
F32, BF16, I32 = jnp.float32, jnp.bfloat16, jnp.int32

HD = 128
NX = 4
NZ = 8
ROWS = 128
HEADS = 8
SLOTS = 512
HALF = SLOTS // 2
LOCAL = 4096
QROWS = ROWS * HEADS
CHUNK = QROWS // NX
TILES = 8
FAR = 1 << 29
LOW = -1e30
HIDDEN = -2e30
QSCALE = math.log2(math.e) / math.sqrt(HD)


def iota(shape, axis):
    return lax.broadcasted_iota(I32, shape, axis)


def kernel(
    meta_ref, q_ref, k_ref, v_ref, out_ref,
    cache, spare, ring, kk, vv, kkd, vvd, qraw, qp, acc, peak, part, partl, got, gotl, fin, gath,
    table, slots, ohf,
    load_sem, swap_s, swap_r, ring_s, ring_r, q_s, q_r, ret_s, ret_r, retl_s, retl_r,
    a2a_s, a2a_r, tx_s, tx_r, tz_s, tz_r,
):
    c = lax.axis_index("context")
    x = lax.div(c, NZ)
    z = lax.rem(c, NZ)
    mirror = NX - 1 - x

    def at(xx, zz):
        return {"context": xx * NZ + zz}

    def xplus(n):
        return lax.rem(x + n, NX)

    def zplus(n):
        return lax.rem(z + n, NZ)

    def remote(src, dst, send, recv, to):
        return pltpu.make_async_remote_copy(
            src_ref=src, dst_ref=dst, send_sem=send, recv_sem=recv, device_id=to, device_id_type=MESH
        )

    barrier = pltpu.get_barrier_semaphore()
    for n in range(1, NX):
        pl.semaphore_signal(barrier, inc=1, device_id=at(xplus(n), z), device_id_type=MESH)
    for n in range(1, NZ):
        pl.semaphore_signal(barrier, inc=1, device_id=at(x, zplus(n)), device_id_type=MESH)

    loads = []
    for i in range(4):
        rows = pl.ds(i * 1024, 1024)
        for side, ref in enumerate((k_ref, v_ref)):
            copy = pltpu.make_async_copy(
                ref.at[rows], cache.at[rows, pl.ds(side * HD, HD)], load_sem.at[i, side]
            )
            copy.start()
            loads.append(copy)

    meta = meta_ref[...]
    qpos_lane = meta[0:1]
    route_lane = meta[1:2]
    count = meta[6:7]
    eye = iota((128, 128), 0) == iota((128, 128), 1)

    def column(row):
        return jnp.sum(jnp.where(eye, row.astype(F32), 0.0), axis=1, keepdims=True).astype(I32)

    def gather(half):
        index = jnp.concatenate([column(meta[2 + 2 * half:3 + 2 * half]), column(meta[3 + 2 * half:4 + 2 * half])], 0)
        total = jnp.zeros((HALF, 2 * HD), F32)
        for i in range(4):
            if half == 1:
                loads[2 * i].wait()
                loads[2 * i + 1].wait()
            hit = iota((HALF, 1024), 1) == index - 1024 * i
            one = jnp.where(hit, 1.0, 0.0).astype(BF16)
            total += jnp.dot(one, cache[pl.ds(i * 1024, 1024), :], preferred_element_type=F32)
        live = iota((HALF, HD), 0) + HALF * half < count
        return jnp.concatenate([total[:, :HD], jnp.where(live, total[:, HD:], 0.0)], 1).astype(BF16)

    spare[...] = gather(1)
    pl.semaphore_wait(barrier, NX - 1 + NZ - 1)
    swap = remote(spare, ring.at[0, 1], swap_s, swap_r, at(mirror, z))
    swap.start()
    ring[0, 0] = gather(0)
    right, left = at(x, zplus(1)), at(x, zplus(NZ - 1))

    def pass_right(source, target):
        return remote(ring.at[source, 0], ring.at[target, 0], ring_s.at[target, 0], ring_r.at[target, 0], right)

    def pass_left(source, target):
        return remote(ring.at[source, 1], ring.at[target, 1], ring_s.at[target, 1], ring_r.at[target, 1], left)

    def own_pass(half, target):
        return (
            remote(ring.at[0, half], ring.at[target, 0], ring_s.at[target, 0], ring_r.at[target, 0], right),
            remote(ring.at[0, half], ring.at[target, 1], ring_s.at[target, 1], ring_r.at[target, 1], left),
        )

    for copy in own_pass(0, 1):
        copy.start()

    dest_lane = lax.div(route_lane, ROWS)
    dest_col = column(dest_lane)
    same = dest_col == dest_lane
    first = iota((128, 128), 0)
    second = iota((128, 128), 1)
    before_lane = jnp.sum(jnp.where(same & (first < second), 1.0, 0.0), axis=0, keepdims=True).astype(I32)
    before_col = jnp.sum(jnp.where(same & (second < first), 1.0, 0.0), axis=1, keepdims=True).astype(I32)
    rank_lane = dest_lane * (ROWS // (NX * NZ)) + before_lane
    rank_col = dest_col * (ROWS // (NX * NZ)) + before_col
    slot_col = column(lax.rem(route_lane, ROWS)).astype(F32)
    slot_row = jnp.sum(jnp.where(rank_col == second, slot_col, 0.0), axis=0, keepdims=True).astype(I32)
    table[z, x] = slot_row + ROWS * count

    def table_x(n):
        return remote(table.at[z, x], table.at[z, x], tx_s.at[n], tx_r.at[n], at(xplus(n), z))

    for n in range(1, NX):
        table_x(n).start()

    stacked = jnp.concatenate([q_ref[:, h * HD:(h + 1) * HD] for h in range(HEADS)], 0)
    rank_key = jnp.concatenate([rank_lane + ROWS * h for h in range(HEADS)], 1)
    within = iota((CHUNK, 1), 0)
    place = lax.div(within, 32) * 4 + lax.rem(within, 4)
    head_of = lax.rem(lax.div(within, 4), HEADS)
    for i in range(NX):
        hit = rank_key == place + 32 * i + ROWS * head_of
        one = jnp.where(hit, 1.0, 0.0).astype(BF16)
        qraw[x, i] = jnp.dot(one, stacked, preferred_element_type=F32).astype(BF16)

    q_right, q_left = at(xplus(1), z), at(xplus(NX - 1), z)

    def q_send(owner, half, number, to):
        view = qraw.at[owner, pl.ds(2 * half, 2)]
        return remote(view, view, q_s.at[number], q_r.at[number], to)

    q_copies = [
        q_send(x, 0, 0, q_right), q_send(x, 1, 3, q_left),
        q_send(x, 1, 1, q_right), q_send(x, 0, 2, q_left),
    ]
    for copy in q_copies:
        copy.start()

    def split_queries(owner):
        for i in range(NX):
            scaled = qraw[owner, i].astype(F32) * QSCALE
            high = scaled.astype(BF16)
            low = (scaled - high.astype(F32)).astype(BF16)
            qp[owner, i] = jnp.concatenate([high, low], 1)

    split_queries(x)
    for n in range(1, NX):
        acc[xplus(n)] = jnp.zeros((NX, CHUNK, 2 * HD), F32)
        peak[xplus(n)] = jnp.full((NX, CHUNK, HD), LOW, F32)

    def keys_of(block):
        keys = jnp.transpose(block[:, :HD])
        return jnp.concatenate([keys, keys], 0)

    def values_of(block, live):
        return jnp.concatenate([block[:, HD:], jnp.where(live, 1.0, 0.0).astype(BF16)], 1)

    whole = jnp.concatenate([ring[0, 0], spare[...]], 0)
    kkd[...] = keys_of(whole)
    vvd[...] = values_of(whole, iota((SLOTS, HD), 0) < count)
    lane = iota((1, SLOTS), 1)
    count_wide = jnp.concatenate([count] * 4, 1)
    key_pos = jnp.where(lane < count_wide, jnp.concatenate([meta[i:i + 1] for i in range(2, 6)], 1), FAR)
    for i in range(NX):
        own_pos = jnp.sum(
            jnp.where(rank_lane == place + 32 * i, qpos_lane.astype(F32), 0.0), axis=1, keepdims=True
        ).astype(I32)
        scores = jnp.dot(qp[x, i], kkd[...], preferred_element_type=F32)
        scores = jnp.where(key_pos <= own_pos, scores, HIDDEN)
        new_peak = jnp.maximum(jnp.max(scores, axis=1, keepdims=True), LOW)
        weights = jnp.exp2(scores - new_peak).astype(BF16)
        acc[x, i] = jnp.dot(weights, vvd[...], preferred_element_type=F32)
        peak[x, i] = jnp.broadcast_to(new_peak, (CHUNK, HD))

    swap.wait_recv()
    for copy in own_pass(1, 2):
        copy.start()

    for n in range(1, NX):
        table_x(n).wait_recv()

    def table_z(n):
        return remote(table.at[z], table.at[z], tz_s.at[n], tz_r.at[n], at(x, zplus(n)))

    for n in range(1, NZ):
        table_z(n).start()

    def halves_of(t):
        step = lax.div(t + 1, 2)
        odd = lax.rem(t, 2) == 1
        ends = (t == 0) | (t == TILES - 1)
        group0 = jnp.where(ends | odd, x, mirror)
        group1 = jnp.where(ends | (~odd), mirror, x)
        shift0 = jnp.where(ends | odd, 0, HALF)
        shift1 = jnp.where(ends | (~odd), HALF, 0)
        return (group0, lax.rem(z - step + NZ, NZ), shift0), (group1, lax.rem(z + step, NZ), shift1)

    def prepare(t):
        block = ring[t].reshape(SLOTS, 2 * HD)
        kk[t] = keys_of(block)
        lives = []
        for group, origin, shift in halves_of(t):
            live_count = lax.div(table[origin, group], ROWS)
            lives.append(iota((HALF, HD), 0) + shift < live_count)
        vv[t] = values_of(block, jnp.concatenate(lives, 0))

    prepare(0)

    def seen(owner, half):
        group, origin, shift = half
        return (owner > group) | ((owner == group) & (origin < z))

    def attend(t, owner):
        half0, half1 = halves_of(t)
        seen0, seen1 = seen(owner, half0), seen(owner, half1)

        @pl.when(seen0 | seen1)
        def _():
            bias0 = jnp.where(seen0, 0.0, HIDDEN)
            bias1 = jnp.where(seen1, 0.0, HIDDEN)
            bias = jnp.where(lane < HALF, bias0, bias1)
            for i in range(NX):
                scores = jnp.dot(qp[owner, i], kk[t], preferred_element_type=F32) + bias
                old_peak = peak[owner, i]
                new_peak = jnp.maximum(jnp.max(scores, axis=1, keepdims=True), old_peak)
                weights = jnp.exp2(scores - new_peak[:, :1]).astype(BF16)
                scale = jnp.exp2(old_peak - new_peak)
                summed = jnp.dot(weights, vv[t], preferred_element_type=F32)
                acc[owner, i] = acc[owner, i] * jnp.concatenate([scale, scale], 1) + summed
                peak[owner, i] = new_peak

    def takes_part(source, owner):
        return jnp.minimum(source, NX - 1 - source) <= owner

    def ret(n, owner):
        xd = xplus(n)
        return (
            remote(part.at[owner, xd], got.at[x, owner], ret_s.at[n, owner], ret_r.at[n, owner], at(xd, z)),
            remote(partl.at[xd, owner], gotl.at[x, owner], retl_s.at[n, owner], retl_r.at[n, owner], at(xd, z)),
        )

    def finish(owner):
        for i in range(NX):
            top = acc[owner, i][:, :HD]
            bottom = acc[owner, i][:, HD:]
            alive = bottom > 0.0
            safe = jnp.where(alive, bottom, 1.0)
            part[owner, i] = (top / safe).astype(BF16)
            logs = jnp.where(alive, peak[owner, i] + jnp.log(safe) * math.log2(math.e), LOW)
            for j in range(2):
                partl[i, owner, j] = jnp.sum(
                    jnp.where(eye, logs[j * 128:(j + 1) * 128], 0.0), axis=0, keepdims=True
                )

        @pl.when(takes_part(x, owner))
        def _():
            for n in range(1, NX):
                for copy in ret(n, owner):
                    copy.start()

        got[x, owner] = part[owner, x]
        gotl[x, owner] = partl[x, owner]

    def one_step(t, carry):
        pass_right(t, t).wait_recv()
        pass_left(t, t).wait_recv()

        @pl.when(t <= 5)
        def _():
            pass_right(t, t + 2).start()

        @pl.when((t <= 4) | (t == 6))
        def _():
            pass_left(t, jnp.minimum(t + 2, TILES - 1)).start()

        @pl.when(t == 1)
        def _():
            q_send(xplus(NX - 1), 0, 0, q_right).wait_recv()
            q_send(xplus(NX - 1), 0, 4, q_right).start()
            q_send(xplus(1), 1, 3, q_left).wait_recv()
            q_send(xplus(1), 1, 5, q_left).start()
            for n in range(1, NZ):
                table_z(n).wait_recv()

        @pl.when(t == 2)
        def _():
            q_send(xplus(NX - 1), 1, 1, q_right).wait_recv()
            q_send(xplus(1), 0, 2, q_left).wait_recv()
            split_queries(xplus(1))
            split_queries(xplus(NX - 1))

        @pl.when(t == 3)
        def _():
            q_send(xplus(2), 0, 4, q_right).wait_recv()
            q_send(xplus(2), 1, 5, q_left).wait_recv()
            split_queries(xplus(2))

        prepare(t)

        def one_owner(n, inner):
            owner = xplus(n)
            ready = jnp.where(n == 0, 1, jnp.where(n == 2, 3, 2))
            lowest = jnp.where(t < ready, t + 1, jnp.where(t == ready, 0, t))

            def one_tile(u, innermost):
                attend(u, owner)
                return innermost

            lax.fori_loop(lowest, t + 1, one_tile, 0)

            @pl.when(t == TILES - 1)
            def _():
                finish(owner)

            return inner

        lax.fori_loop(0, NX, one_owner, 0)
        return carry

    lax.fori_loop(1, TILES, one_step, 0)

    def rows_of(row):
        return jnp.sum(jnp.where(eye, row, 0.0), axis=1, keepdims=True)

    for owner in range(NX):
        sources = [s for s in range(NX) if min(s, NX - 1 - s) <= owner]
        for n in range(1, NX):
            @pl.when(takes_part(xplus(NX - n), owner))
            def _():
                for copy in ret(n, owner):
                    copy.wait_recv()
        logs = [
            jnp.concatenate([rows_of(gotl[s, owner, j]) for j in range(2)], 0) for s in sources
        ]
        most = logs[0]
        for value in logs[1:]:
            most = jnp.maximum(most, value)
        total = jnp.zeros((CHUNK, HD), F32)
        weight = jnp.zeros((CHUNK, 1), F32)
        for s, value in zip(sources, logs):
            share = jnp.exp2(value - most)
            weight = weight + share
            total = total + share * got[s, owner].astype(F32)
        fin[owner] = (total / weight).astype(BF16).reshape(NZ, CHUNK // NZ, HD)

    def spread(n):
        zd = zplus(n)
        return remote(fin.at[:, zd], gath.at[z], a2a_s.at[n], a2a_r.at[n], at(x, zd))

    for n in range(1, NZ):
        spread(n).start()
    gath[z] = fin[:, z]

    for zz in range(NZ):
        for xx in range(NX):
            slots[zz * NX + xx:zz * NX + xx + 1, :] = lax.rem(table[zz, xx], ROWS).astype(F32)
    wide = iota((128, QROWS), 1)
    pick = jnp.where(iota((128, QROWS), 0) == c * 4 + lax.rem(wide, 4), 1.0, 0.0).astype(BF16)
    picked = jnp.dot(slots[...].astype(BF16), pick, preferred_element_type=F32)
    mine = iota((32, QROWS), 0) == lax.div(iota((32, QROWS), 1), 32)
    slot_of = jnp.sum(jnp.where(mine, picked, 0.0), axis=0, keepdims=True).astype(I32)
    lanes = iota((1, QROWS), 1)
    key = slot_of + ROWS * lax.rem(lax.div(lanes, 4), HEADS)
    for h in range(HEADS):
        hit = iota((ROWS, QROWS), 0) + ROWS * h == key
        ohf[h] = jnp.where(hit, 1.0, 0.0).astype(BF16)

    for n in range(1, NZ):
        spread(n).wait_recv()
    arrived = gath[...].reshape(QROWS, HD)
    for h in range(HEADS):
        out_ref[:, h * HD:(h + 1) * HD] = jnp.dot(
            ohf[h], arrived, preferred_element_type=F32
        ).astype(BF16)

    swap.wait_send()
    for copy in own_pass(0, 1) + own_pass(1, 2):
        copy.wait_send()
    for t in range(1, 6):
        pass_right(t, t + 2).wait_send()
    for t in (1, 2, 3, 4, 6):
        pass_left(t, min(t + 2, TILES - 1)).wait_send()
    for copy in q_copies:
        copy.wait_send()
    q_send(xplus(NX - 1), 0, 4, q_right).wait_send()
    q_send(xplus(1), 1, 5, q_left).wait_send()
    for n in range(1, NX):
        table_x(n).wait_send()
        for owner in range(NX):
            @pl.when(takes_part(x, owner))
            def _():
                for copy in ret(n, owner):
                    copy.wait_send()
    for n in range(1, NZ):
        table_z(n).wait_send()
        spread(n).wait_send()


def per_device(queries, query_pos, k_cache, v_cache, kept_index, kept_count, route):
    device_index = lax.axis_index("context")
    live = jnp.arange(SLOTS, dtype=I32) < kept_count[0]
    index = jnp.where(live, kept_index, kept_index[0])
    meta = jnp.concatenate(
        [
            (query_pos - device_index * LOCAL)[None],
            route[None],
            index.reshape(4, 128),
            jnp.broadcast_to(kept_count[0], (2, 128)),
        ],
        0,
    )
    dma = pltpu.SemaphoreType.DMA
    vmem = pltpu.VMEM
    return pl.pallas_call(
        kernel,
        out_shape=jax.ShapeDtypeStruct((ROWS, QROWS), BF16),
        in_specs=[
            pl.BlockSpec(memory_space=vmem),
            pl.BlockSpec(memory_space=vmem),
            pl.BlockSpec(memory_space=pl.ANY),
            pl.BlockSpec(memory_space=pl.ANY),
        ],
        out_specs=pl.BlockSpec(memory_space=vmem),
        scratch_shapes=[
            vmem((LOCAL, 2 * HD), BF16),
            vmem((HALF, 2 * HD), BF16),
            vmem((TILES, 2, HALF, 2 * HD), BF16),
            vmem((TILES, 2 * HD, SLOTS), BF16),
            vmem((TILES, SLOTS, 2 * HD), BF16),
            vmem((2 * HD, SLOTS), BF16),
            vmem((SLOTS, 2 * HD), BF16),
            vmem((NX, NX, CHUNK, HD), BF16),
            vmem((NX, NX, CHUNK, 2 * HD), BF16),
            vmem((NX, NX, CHUNK, 2 * HD), F32),
            vmem((NX, NX, CHUNK, HD), F32),
            vmem((NX, NX, CHUNK, HD), BF16),
            vmem((NX, NX, 2, 1, 128), F32),
            vmem((NX, NX, CHUNK, HD), BF16),
            vmem((NX, NX, 2, 1, 128), F32),
            vmem((NX, NZ, CHUNK // NZ, HD), BF16),
            vmem((NZ, NX, CHUNK // NZ, HD), BF16),
            vmem((NZ, NX, 1, 128), I32),
            vmem((NZ * NX, 128), F32),
            vmem((HEADS, ROWS, QROWS), BF16),
            dma((4, 2)), dma, dma,
            dma((TILES, 2)), dma((TILES, 2)),
            dma((6,)), dma((6,)),
            dma((NX, NX)), dma((NX, NX)), dma((NX, NX)), dma((NX, NX)),
            dma((NZ,)), dma((NZ,)),
            dma((NX,)), dma((NX,)),
            dma((NZ,)), dma((NZ,)),
        ],
        compiler_params=pltpu.CompilerParams(
            collective_id=0, has_side_effects=True, vmem_limit_bytes=56 * 1024 * 1024
        ),
    )(meta, queries, k_cache, v_cache)


def solution(mesh):
    placed = (
        P("context", "mp"),
        P("context"),
        P("context", "mp"),
        P("context", "mp"),
        P("context"),
        P("context"),
        P("context"),
    )
    return jax.shard_map(
        per_device, mesh=mesh, in_specs=placed, out_specs=P("context", "mp"), check_vma=False
    )
```

time: 351 us -> 78.5 us (0.22)
  waiting for transfers between devices: 109 us -> 0 us
  Pallas kernels: 0 us -> 72.7 us
  blocking collectives: 48.2 us -> 0 us
  starting transfers between devices: 48.1 us -> 0 us
  loops' own time: 43.4 us -> 0 us
  other arithmetic: 33.6 us -> 1.33 us
  local copies, waits for them, and re-layouts: 28.8 us -> 3.59 us
  matrix products: 22.9 us -> 0 us
  between operations: 14.3 us -> 0.69 us
    all_gather x2 -> x0, waiting for transfers between devices: 98.9 us -> none  [the longest x1 81.7 us: attend(): value_piece = lax.all_gather(kept_vals, 'context', axis=0, tiled=True)]
    pallas_call x0 -> x1, Pallas kernels: none -> 72.7 us  [per_device(): pl.pallas_call(kernel, out_shape=jax.ShapeDtypeStruct((ROWS, QROWS), BF16...]
    all_gather x1 -> x0, blocking collectives: 48.2 us -> none  [attend(): pos_piece = lax.all_gather(key_pos, 'context', axis=0, tiled=True)]
    all_to_all x2 -> x0, starting transfers between devices: 48 us -> none  [the longest x1 36.5 us: per_device(): lax.all_to_all(attended[send_order], 'context', split_axis=0, concat_axis...]
    another operation x33 -> x0, loops' own time: 43.4 us -> none  [the longest x1 42.3 us: attend(): lax.fori_loop(0, tile_count, tile_step, initial)]
    dot_general x36 -> x0, matrix products: 22.9 us -> none  [the longest x18 12.8 us: weigh_values(): jnp.einsum('qhgk,khd->qhgd', weights_bf.reshape(row_total, kv_heads, grou...]
    dynamic_slice x16 -> x0, local copies, waits for them, and re-layouts: 17 us -> none  [tile_step(): lax.dynamic_slice_in_dim(value_piece, step_index * tile_rows, tile_rows, 0)]
    reduce_sum x18 -> x0, other arithmetic: 12.4 us -> none  [block_update(): denominator = denominator * rescale + jnp.sum(weights, axis=-1)]
  transfers between devices with their start and end apart: 4 -> 0, of which waited for: 3 -> 0; matrix products, arithmetic and copies ran while one was open for 22% -> 0% of each run, Pallas kernels for 0% -> 0%
where the time goes in v1:
time: 78.5 us; the launch traced here: 78.4 us
  Pallas kernels  72.7 us (93%)
  local copies, waits for them, and re-layouts  3.59 us (5%)
  other arithmetic  1.33 us (2%)
    pallas_call x1, Pallas kernels, per_device(): pl.pallas_call(kernel, out_shape=jax.ShapeDtypeStruct((ROWS, QROWS), BF16...  72.7 us
    unnamed x7, local copies, waits for them, and re-layouts  3 us

profile of v1, /device:TPU:20, one launch (start us, length us, event | category | flops | bytes accessed | tf_op | source)
XLA Modules:
  0.0 78.4 jit_solution(9333806920695381872)
XLA Ops:
  0.7 0.0 copy-start
  0.7 0.7 copy-done
  1.3 0.5 slice.3
  1.8 0.0 copy-start.2
  1.8 0.7 copy-done.2
  2.5 0.1 pad.3.clone
  2.6 0.0 copy-start.1
  2.6 0.7 select_bitcast_fusion
  3.3 0.0 copy-done.1
  3.3 0.7 add_add_fusion.meta_ref
  3.9 72.7 %shard_map.73 = bf16[128,1024]{1,0:T(8,128)(2,1)} custom-call(s32[8,128]{1,0:T(8,128)} %add_add_fusion.meta_ref, bf16[128,1024]{1,0:T(8,128)(2,1)} %q_ref.1, bf16[4096,128]{1,0:T(8,128)(2,1)} %k_ref.1, bf16[4096,128]{1,0:T(8,128)(2,1)} %v_ref.1), custom_call_target="tpu_custom_call" | custom-call | tf_op jit(solution)/shard_map/pallas_call | solution.py:437
  76.7 1.7 %copy.10 = bf16[128,1024]{1,0:T(8,128)(2,1)} copy(bf16[128,1024]{1,0:T(8,128)(2,1)} %shard_map.73) | data formatting | bytes 524288
  (2 shorter events, 0.0 us)
Async XLA Ops:
  0.7 0.7 copy-start
  1.8 0.7 copy-start.2
  2.6 0.7 copy-start.1

commit v2 on v1

v2 whole, which is shorter than its diff:
```python
import math

import jax
import jax.numpy as jnp
from jax import lax
from jax.experimental import pallas as pl
from jax.experimental.pallas import tpu as pltpu
from jax.sharding import PartitionSpec as P

MESH = pl.DeviceIdType.MESH
F32, BF16, I32 = jnp.float32, jnp.bfloat16, jnp.int32

HD = 128
NX = 4
NZ = 8
ROWS = 128
HEADS = 8
SLOTS = 512
HALF = SLOTS // 2
LOCAL = 4096
QROWS = ROWS * HEADS
CHUNK = QROWS // NX
TILES = 8
FAR = 1 << 29
LOW = -1e30
HIDDEN = -2e30
QSCALE = math.log2(math.e) / math.sqrt(HD)


def iota(shape, axis):
    return lax.broadcasted_iota(I32, shape, axis)


def kernel(
    idx_hbm, route_hbm, qpos_hbm, q_hbm, k_hbm, v_hbm, count_ref, out_ref,
    cache, hot, idx_ref, route_ref, qpos_ref, q_ref,
    spare, ring, kk, vv, kkd, vvd, qraw, qp, acc, peak, part, partl, got, gotl, fin, gath,
    table, slots, ohf,
    load_sem, small_sem, swap_s, swap_r, ring_s, ring_r, q_s, q_r, ret_s, ret_r, retl_s, retl_r,
    a2a_s, a2a_r, tx_s, tx_r, tz_s, tz_r,
):
    c = lax.axis_index("context")
    x = lax.div(c, NZ)
    z = lax.rem(c, NZ)
    mirror = NX - 1 - x
    right, left = (x, lax.rem(z + 1, NZ)), (x, lax.rem(z + NZ - 1, NZ))

    def at(where):
        return {"context": where[0] * NZ + where[1]}

    def xplus(n):
        return lax.rem(x + n, NX)

    def zplus(n):
        return lax.rem(z + n, NZ)

    def remote(src, dst, send, recv, to):
        return pltpu.make_async_remote_copy(
            src_ref=src, dst_ref=dst, send_sem=send, recv_sem=recv, device_id=at(to), device_id_type=MESH
        )

    smalls = []
    for i, (src, dst) in enumerate(
        ((idx_hbm, idx_ref), (route_hbm, route_ref), (qpos_hbm, qpos_ref), (q_hbm, q_ref))
    ):
        copy = pltpu.make_async_copy(src, dst, small_sem.at[i])
        copy.start()
        smalls.append(copy)
    loads = []
    for i in range(4):
        rows = pl.ds(i * 1024, 1024)
        for side, ref in enumerate((k_hbm, v_hbm)):
            copy = pltpu.make_async_copy(
                ref.at[rows], cache.at[rows, pl.ds(side * HD, HD)], load_sem.at[i, side]
            )
            copy.start()
            loads.append(copy)

    barrier = pltpu.get_barrier_semaphore()
    for n in range(1, NX):
        pl.semaphore_signal(barrier, inc=1, device_id=at((xplus(n), z)), device_id_type=MESH)
    for n in range(1, NZ):
        pl.semaphore_signal(barrier, inc=1, device_id=at((x, zplus(n))), device_id_type=MESH)

    count = count_ref[0]
    eye = iota((128, 128), 0) == iota((128, 128), 1)
    lane = iota((1, 128), 1)

    def column(row):
        return jnp.sum(jnp.where(eye, row.astype(F32), 0.0), axis=1, keepdims=True).astype(I32)

    for copy in smalls[:3]:
        copy.wait()
    kept = idx_ref[...]
    repeat = jnp.broadcast_to(kept[0:1, 0:1], (1, 128))
    for i in (2, 3, 0, 1):
        index = column(jnp.where(lane + 128 * i < count, kept[i:i + 1], repeat))
        for j in range(4):
            hit = iota((128, 1024), 1) == index - 1024 * j
            hot[i * 128:(i + 1) * 128, j * 1024:(j + 1) * 1024] = jnp.where(hit, 1.0, 0.0).astype(BF16)

    route_lane = route_ref[...]
    dest_lane = lax.div(route_lane, ROWS)
    dest_col = column(dest_lane)
    same = dest_col == dest_lane
    first = iota((128, 128), 0)
    second = iota((128, 128), 1)
    before_lane = jnp.sum(jnp.where(same & (first < second), 1.0, 0.0), axis=0, keepdims=True).astype(I32)
    before_col = jnp.sum(jnp.where(same & (second < first), 1.0, 0.0), axis=1, keepdims=True).astype(I32)
    rank_lane = dest_lane * (ROWS // (NX * NZ)) + before_lane
    rank_col = dest_col * (ROWS // (NX * NZ)) + before_col
    slot_col = column(lax.rem(route_lane, ROWS)).astype(F32)
    slot_row = jnp.sum(jnp.where(rank_col == second, slot_col, 0.0), axis=0, keepdims=True).astype(I32)
    table[z, x] = slot_row + ROWS * count

    def gather(half):
        total = jnp.dot(hot[half * HALF:(half + 1) * HALF, :], cache[...], preferred_element_type=F32)
        live = iota((HALF, HD), 0) + HALF * half < count
        keys = jnp.transpose(total[:, :HD].astype(BF16))
        values = jnp.where(live, total[:, HD:], 0.0).astype(BF16)
        return jnp.concatenate([keys, jnp.concatenate([values[:HD], values[HD:]], 1)], 0)

    for copy in loads:
        copy.wait()
    spare[...] = gather(1)
    pl.semaphore_wait(barrier, NX - 1 + NZ - 1)
    swap = remote(spare, ring.at[0, 1], swap_s, swap_r, (mirror, z))
    swap.start()
    ring[0, 0] = gather(0)

    def pass_right(source, target):
        return remote(ring.at[source, 0], ring.at[target, 0], ring_s.at[target, 0], ring_r.at[target, 0], right)

    def pass_left(source, target):
        return remote(ring.at[source, 1], ring.at[target, 1], ring_s.at[target, 1], ring_r.at[target, 1], left)

    def own_pass(half, target):
        return (
            remote(ring.at[0, half], ring.at[target, 0], ring_s.at[target, 0], ring_r.at[target, 0], right),
            remote(ring.at[0, half], ring.at[target, 1], ring_s.at[target, 1], ring_r.at[target, 1], left),
        )

    for copy in own_pass(0, 1):
        copy.start()

    def table_x(n):
        return remote(table.at[z, x], table.at[z, x], tx_s.at[n], tx_r.at[n], (xplus(n), z))

    for n in range(1, NX):
        table_x(n).start()

    smalls[3].wait()
    stacked = jnp.concatenate([q_ref[:, h * HD:(h + 1) * HD] for h in range(HEADS)], 0)
    rank_key = jnp.concatenate([rank_lane + ROWS * h for h in range(HEADS)], 1)
    within = iota((CHUNK, 1), 0)
    place = lax.div(within, 32) * 4 + lax.rem(within, 4)
    head_of = lax.rem(lax.div(within, 4), HEADS)
    for i in range(NX):
        hit = rank_key == place + 32 * i + ROWS * head_of
        one = jnp.where(hit, 1.0, 0.0).astype(BF16)
        qraw[x, i] = jnp.dot(one, stacked, preferred_element_type=F32).astype(BF16)

    q_right, q_left = (xplus(1), z), (xplus(NX - 1), z)

    def q_send(owner, half, number, to):
        view = qraw.at[owner, pl.ds(2 * half, 2)]
        return remote(view, view, q_s.at[number], q_r.at[number], to)

    q_copies = [
        q_send(x, 0, 0, q_right), q_send(x, 1, 3, q_left),
        q_send(x, 1, 1, q_right), q_send(x, 0, 2, q_left),
    ]
    for copy in q_copies:
        copy.start()

    swap.wait_recv()
    for copy in own_pass(1, 2):
        copy.start()

    for n in range(1, NX):
        table_x(n).wait_recv()

    def table_z(n):
        return remote(table.at[z], table.at[z], tz_s.at[n], tz_r.at[n], (x, zplus(n)))

    for n in range(1, NZ):
        table_z(n).start()

    def split_queries(owner):
        for i in range(NX):
            scaled = qraw[owner, i].astype(F32) * QSCALE
            high = scaled.astype(BF16)
            low = (scaled - high.astype(F32)).astype(BF16)
            qp[owner, i] = jnp.concatenate([high, low], 1)

    split_queries(x)
    for n in range(1, NX):
        acc[xplus(n)] = jnp.zeros((NX, CHUNK, 2 * HD), F32)
        peak[xplus(n)] = jnp.full((NX, CHUNK, HD), LOW, F32)

    def keys_of(block):
        return jnp.concatenate([block[:HD], block[:HD]], 0)

    def values_of(block, live):
        mark = jnp.where(live, 1.0, 0.0).astype(BF16)
        return jnp.concatenate([jnp.concatenate([block[HD:, :HD], block[HD:, HD:]], 0), mark], 1)

    slot_wide = iota((HALF, HD), 0)
    for half, block in enumerate((ring[0, 0], spare[...])):
        kkd[:, half * HALF:(half + 1) * HALF] = keys_of(block)
        vvd[half * HALF:(half + 1) * HALF] = values_of(block, slot_wide + HALF * half < count)
    key_pos = jnp.concatenate(
        [jnp.where(lane + 128 * i < count, kept[i:i + 1], FAR) for i in range(4)], 1
    )
    local_pos = (qpos_ref[...] - c * LOCAL).astype(F32)
    scores = [jnp.dot(qp[x, i], kkd[...], preferred_element_type=F32) for i in range(NX)]
    for i in range(NX):
        own_pos = jnp.sum(
            jnp.where(rank_lane == place + 32 * i, local_pos, 0.0), axis=1, keepdims=True
        ).astype(I32)
        seen_scores = jnp.where(key_pos <= own_pos, scores[i], HIDDEN)
        new_peak = jnp.broadcast_to(
            jnp.maximum(jnp.max(seen_scores, axis=1, keepdims=True), LOW), (CHUNK, HD)
        )
        weights = jnp.exp2(seen_scores - jnp.concatenate([new_peak] * 4, 1)).astype(BF16)
        acc[x, i] = jnp.dot(weights, vvd[...], preferred_element_type=F32)
        peak[x, i] = new_peak

    def owner_row(group):
        return jnp.where(group == 0, x, mirror)

    origins = [z] + [zplus(n if h else NZ - n) for n in (1, 2, 3) for h in (0, 1)] + [zplus(4)]

    def prepare(t, side, group, h):
        block = ring[t, side]
        live_count = lax.div(table[origins[h], x if group == 0 else mirror], ROWS)
        kk[group, h] = keys_of(block)
        vv[group, h * HALF:(h + 1) * HALF] = values_of(block, slot_wide + HALF * group < live_count)

    def poll(t):
        pass_right(t, t).wait_recv()
        pass_left(t, t).wait_recv()
        if t <= 5:
            pass_right(t, t + 2).start()
        if t <= 4 or t == 6:
            pass_left(t, min(t + 2, TILES - 1)).start()
        if t == TILES - 1:
            prepare(t, 0, 0, 7)
            prepare(t, 1, 1, 7)
        else:
            h = t if t % 2 else t - 1
            prepare(t, 0, 1 - t % 2, h)
            prepare(t, 1, 1 - t % 2, h + 1)

    def attend(owner, group, halves):
        row = owner_row(group)
        every = owner > row
        visible = [origins[h] < z for h in halves]
        some = visible[0]
        for v in visible[1:]:
            some = some | v

        def update(bias):
            scores = []
            for i in range(NX):
                parts = [jnp.dot(qp[owner, i], kk[group, h], preferred_element_type=F32) for h in halves]
                if bias is not None:
                    parts = [p + b for p, b in zip(parts, bias)]
                scores.append(parts)
            for i in range(NX):
                old_peak = peak[owner, i]
                top = scores[i][0]
                for p in scores[i][1:]:
                    top = jnp.maximum(top, p)
                new_peak = jnp.maximum(jnp.max(top, axis=1, keepdims=True), old_peak)
                twice = jnp.concatenate([new_peak, new_peak], 1)
                weights = jnp.concatenate([jnp.exp2(p - twice).astype(BF16) for p in scores[i]], 1)
                summed = jnp.dot(
                    weights, vv[group, pl.ds(halves[0] * HALF, len(halves) * HALF)], preferred_element_type=F32
                )
                scale = jnp.exp2(old_peak - new_peak)
                acc[owner, i] = acc[owner, i] * jnp.concatenate([scale, scale], 1) + summed
                peak[owner, i] = new_peak

        @pl.when(every)
        def _():
            update(None)

        @pl.when((owner == row) & some)
        def _():
            update([jnp.where(v, 0.0, HIDDEN) for v in visible])

    def takes_part(source, owner):
        return jnp.minimum(source, NX - 1 - source) <= owner

    def ret(n, owner):
        xd = xplus(n)
        return (
            remote(part.at[owner, xd], got.at[x, owner], ret_s.at[n, owner], ret_r.at[n, owner], (xd, z)),
            remote(partl.at[xd, owner], gotl.at[x, owner], retl_s.at[n, owner], retl_r.at[n, owner], (xd, z)),
        )

    def finish(owner):
        for i in range(NX):
            top = acc[owner, i][:, :HD]
            bottom = acc[owner, i][:, HD:]
            alive = bottom > 0.0
            safe = jnp.where(alive, bottom, 1.0)
            part[owner, i] = (top / safe).astype(BF16)
            logs = jnp.where(alive, peak[owner, i] + jnp.log(safe) * math.log2(math.e), LOW)
            for j in range(2):
                partl[i, owner, j] = jnp.sum(
                    jnp.where(eye, logs[j * 128:(j + 1) * 128], 0.0), axis=0, keepdims=True
                )

        @pl.when(takes_part(x, owner))
        def _():
            for n in range(1, NX):
                for copy in ret(n, owner):
                    copy.start()

        got[x, owner] = part[owner, x]
        gotl[x, owner] = partl[x, owner]

    prepare(0, 0, 0, 0)
    prepare(0, 1, 1, 0)

    def destinations():
        for zz in range(NZ):
            for xx in range(NX):
                slots[zz * NX + xx:zz * NX + xx + 1, :] = lax.rem(table[zz, xx], ROWS).astype(F32)
        wide = iota((128, QROWS), 1)
        pick = jnp.where(iota((128, QROWS), 0) == c * 4 + lax.rem(wide, 4), 1.0, 0.0).astype(BF16)
        picked = jnp.dot(slots[...].astype(BF16), pick, preferred_element_type=F32)
        mine = iota((32, QROWS), 0) == lax.div(iota((32, QROWS), 1), 32)
        slot_of = jnp.sum(jnp.where(mine, picked, 0.0), axis=0, keepdims=True).astype(I32)
        lanes = iota((1, QROWS), 1)
        key = slot_of + ROWS * lax.rem(lax.div(lanes, 4), HEADS)
        for h in range(HEADS):
            hit = iota((ROWS, QROWS), 0) + ROWS * h == key
            ohf[h] = jnp.where(hit, 1.0, 0.0).astype(BF16)

    def early(w, carry):
        @pl.when(w == 0)
        def _():
            for n in range(1, NZ):
                table_z(n).wait_recv()
            poll(1)

        @pl.when(w == 1)
        def _():
            q_send(xplus(NX - 1), 0, 0, q_right).wait_recv()
            q_send(xplus(NX - 1), 0, 4, q_right).start()
            q_send(xplus(1), 1, 3, q_left).wait_recv()
            q_send(xplus(1), 1, 5, q_left).start()
            destinations()
            poll(2)

        @pl.when(w == 2)
        def _():
            q_send(xplus(NX - 1), 1, 1, q_right).wait_recv()
            q_send(xplus(1), 0, 2, q_left).wait_recv()
            split_queries(xplus(1))
            split_queries(xplus(NX - 1))

        @pl.when(w == 4)
        def _():
            poll(3)

        @pl.when(w == 6)
        def _():
            poll(4)
            q_send(xplus(2), 0, 4, q_right).wait_recv()
            q_send(xplus(2), 1, 5, q_left).wait_recv()
            split_queries(xplus(2))

        turn = lax.div(w, 2)
        n = jnp.where(turn == 2, 3, jnp.where(turn == 3, 2, turn))
        attend(xplus(n), lax.rem(w, 2), (0, 1, 2))
        return carry

    lax.fori_loop(0, 2 * NX, early, 0)
    poll(5)

    def late(i, carry):
        @pl.when(i < NX)
        def _():
            def one(group, inner):
                @pl.when((i == 0) & (group == 1))
                def _():
                    poll(6)

                attend(NX - 1 - i, group, (3, 4, 5, 6))
                return inner

            lax.fori_loop(0, 2, one, 0)

        @pl.when(i == 0)
        def _():
            poll(7)

        @pl.when(i >= 1)
        def _():
            def one(group, inner):
                attend(NX - i, group, (7,))
                return inner

            lax.fori_loop(0, 2, one, 0)
            finish(NX - i)

        return carry

    lax.fori_loop(0, NX + 1, late, 0)

    def rows_of(row):
        return jnp.sum(jnp.where(eye, row, 0.0), axis=1, keepdims=True)

    def spread(n, owner):
        zd = zplus(n)
        return remote(fin.at[owner, zd], gath.at[z, owner], a2a_s.at[owner, n], a2a_r.at[owner, n], (x, zd))

    for owner in range(NX - 1, -1, -1):
        sources = [s for s in range(NX) if min(s, NX - 1 - s) <= owner]
        for n in range(1, NX):
            @pl.when(takes_part(xplus(NX - n), owner))
            def _():
                for copy in ret(n, owner):
                    copy.wait_recv()
        logs = [
            jnp.concatenate([rows_of(gotl[s, owner, j]) for j in range(2)], 0) for s in sources
        ]
        most = logs[0]
        for value in logs[1:]:
            most = jnp.maximum(most, value)
        total = jnp.zeros((CHUNK, HD), F32)
        weight = jnp.zeros((CHUNK, 1), F32)
        for s, value in zip(sources, logs):
            share = jnp.exp2(value - most)
            weight = weight + share
            total = total + share * got[s, owner].astype(F32)
        fin[owner] = (total / weight).astype(BF16).reshape(NZ, CHUNK // NZ, HD)
        for n in range(1, NZ):
            spread(n, owner).start()
        gath[z, owner] = fin[owner, z]

    for owner in range(NX - 1, -1, -1):
        for n in range(1, NZ):
            spread(n, owner).wait_recv()
    arrived = gath[...].reshape(QROWS, HD)
    for h in range(HEADS):
        out_ref[:, h * HD:(h + 1) * HD] = jnp.dot(
            ohf[h], arrived, preferred_element_type=F32
        ).astype(BF16)

    swap.wait_send()
    for copy in own_pass(0, 1) + own_pass(1, 2):
        copy.wait_send()
    for t in range(1, 6):
        pass_right(t, t + 2).wait_send()
    for t in (1, 2, 3, 4, 6):
        pass_left(t, min(t + 2, TILES - 1)).wait_send()
    for copy in q_copies:
        copy.wait_send()
    q_send(xplus(NX - 1), 0, 4, q_right).wait_send()
    q_send(xplus(1), 1, 5, q_left).wait_send()
    for n in range(1, NX):
        table_x(n).wait_send()
        for owner in range(NX):
            @pl.when(takes_part(x, owner))
            def _():
                for copy in ret(n, owner):
                    copy.wait_send()
    for n in range(1, NZ):
        table_z(n).wait_send()
        for owner in range(NX):
            spread(n, owner).wait_send()


def per_device(queries, query_pos, k_cache, v_cache, kept_index, kept_count, route):
    dma = pltpu.SemaphoreType.DMA
    vmem = pltpu.VMEM
    anywhere = pl.BlockSpec(memory_space=pl.ANY)
    return pl.pallas_call(
        kernel,
        out_shape=jax.ShapeDtypeStruct((ROWS, QROWS), BF16),
        in_specs=[anywhere] * 6 + [pl.BlockSpec(memory_space=pltpu.SMEM)],
        out_specs=pl.BlockSpec(memory_space=vmem),
        scratch_shapes=[
            vmem((LOCAL, 2 * HD), BF16),
            vmem((SLOTS, LOCAL), BF16),
            vmem((4, 128), I32),
            vmem((1, 128), I32),
            vmem((1, 128), I32),
            vmem((ROWS, QROWS), BF16),
            vmem((HALF, 2 * HD), BF16),
            vmem((TILES, 2, HALF, 2 * HD), BF16),
            vmem((2, TILES, 2 * HD, HALF), BF16),
            vmem((2, TILES * HALF, 2 * HD), BF16),
            vmem((2 * HD, SLOTS), BF16),
            vmem((SLOTS, 2 * HD), BF16),
            vmem((NX, NX, CHUNK, HD), BF16),
            vmem((NX, NX, CHUNK, 2 * HD), BF16),
            vmem((NX, NX, CHUNK, 2 * HD), F32),
            vmem((NX, NX, CHUNK, HD), F32),
            vmem((NX, NX, CHUNK, HD), BF16),
            vmem((NX, NX, 2, 1, 128), F32),
            vmem((NX, NX, CHUNK, HD), BF16),
            vmem((NX, NX, 2, 1, 128), F32),
            vmem((NX, NZ, CHUNK // NZ, HD), BF16),
            vmem((NZ, NX, CHUNK // NZ, HD), BF16),
            vmem((NZ, NX, 1, 128), I32),
            vmem((NZ * NX, 128), F32),
            vmem((HEADS, ROWS, QROWS), BF16),
            dma((4, 2)), dma((4,)), dma, dma,
            dma((TILES, 2)), dma((TILES, 2)),
            dma((6,)), dma((6,)),
            dma((NX, NX)), dma((NX, NX)), dma((NX, NX)), dma((NX, NX)),
            dma((NX, NZ)), dma((NX, NZ)),
            dma((NX,)), dma((NX,)),
            dma((NZ,)), dma((NZ,)),
        ],
        compiler_params=pltpu.CompilerParams(
            collective_id=0, has_side_effects=True, vmem_limit_bytes=56 * 1024 * 1024
        ),
    )(
        kept_index.reshape(4, 128), route.reshape(1, 128), query_pos.reshape(1, 128),
        queries, k_cache, v_cache, kept_count,
    )


def solution(mesh):
    placed = (
        P("context", "mp"),
        P("context"),
        P("context", "mp"),
        P("context", "mp"),
        P("context"),
        P("context"),
        P("context"),
    )
    return jax.shard_map(
        per_device, mesh=mesh, in_specs=placed, out_specs=P("context", "mp"), check_vma=False
    )
```

time: 78.5 us -> 63.1 us (0.80)
  Pallas kernels: 72.7 us -> 60.1 us
  local copies, waits for them, and re-layouts: 3.59 us -> 1.67 us
  other arithmetic: 1.33 us -> 0 us
    pallas_call x1, Pallas kernels: 72.7 us -> 60.1 us  [per_device(): pl.pallas_call(kernel, out_shape=jax.ShapeDtypeStruct((ROWS, QROWS), BF16...]
    unnamed x7 -> x1, local copies, waits for them, and re-layouts: 3 us -> 1.67 us
where the time goes in v2:
time: 63.1 us; the launch traced here: 62.4 us
  Pallas kernels  60.1 us (95%)
  local copies, waits for them, and re-layouts  1.67 us (3%)
  between operations  0.66 us (1%)
    pallas_call x1, Pallas kernels, per_device(): pl.pallas_call(kernel, out_shape=jax.ShapeDtypeStruct((ROWS, QROWS), BF16...  60.1 us
    unnamed x1, local copies, waits for them, and re-layouts  1.67 us

profile of v2, /device:TPU:20, one launch (start us, length us, event | category | flops | bytes accessed | tf_op | source)
XLA Modules:
  0.0 62.4 jit_solution(16672356350103457997)
XLA Ops:
  0.7 60.1 %shard_map.73 = bf16[128,1024]{1,0:T(8,128)(2,1)} custom-call(s32[4,128]{1,0:T(4,128)} %bitcast.3, s32[1,128]{1,0:T(1,128)} %bitcast.4, s32[1,128]{1,0:T(1,128)} %bitcast.5, bf16[128,1024]{1,0:T(8,128)(2,1)} %q_hbm.1, bf16[4096,128]{1,0:T(8,128)(2,1)} %k_hbm.1, bf16[4096,128]{1,0:T(8,128)(2,1)} %v_hbm.1, s32[1]{0:T(128)S(6)} %copy.9.count_ref), custom_call_target="tpu_custom_call" | custom-call | tf_op jit(solution)/shard_map/pallas_call | solution.py:483
  60.8 1.7 %copy.10 = bf16[128,1024]{1,0:T(8,128)(2,1)} copy(bf16[128,1024]{1,0:T(8,128)(2,1)} %shard_map.73) | data formatting | bytes 524288

commit v3 on v2

--- a/solution.py
+++ b/solution.py
@@ -229,33 +229,40 @@
     def owner_row(group):
         return jnp.where(group == 0, x, mirror)
 
-    origins = [z] + [zplus(n if h else NZ - n) for n in (1, 2, 3) for h in (0, 1)] + [zplus(4)]
+    def origin_of(h):
+        step = lax.div(h + 1, 2)
+        return lax.rem(jnp.where(lax.rem(h, 2) == 1, z + NZ - step, z + step), NZ)
 
     def prepare(t, side, group, h):
         block = ring[t, side]
-        live_count = lax.div(table[origins[h], x if group == 0 else mirror], ROWS)
+        live_count = lax.div(table[origin_of(h), owner_row(group)], ROWS)
         kk[group, h] = keys_of(block)
-        vv[group, h * HALF:(h + 1) * HALF] = values_of(block, slot_wide + HALF * group < live_count)
-
-    def poll(t):
+        vv[group, pl.ds(h * HALF, HALF)] = values_of(block, slot_wide + HALF * group < live_count)
+
+    def forward(t):
         pass_right(t, t).wait_recv()
         pass_left(t, t).wait_recv()
-        if t <= 5:
+
+        @pl.when(t <= 5)
+        def _():
             pass_right(t, t + 2).start()
-        if t <= 4 or t == 6:
-            pass_left(t, min(t + 2, TILES - 1)).start()
-        if t == TILES - 1:
-            prepare(t, 0, 0, 7)
-            prepare(t, 1, 1, 7)
-        else:
-            h = t if t % 2 else t - 1
-            prepare(t, 0, 1 - t % 2, h)
-            prepare(t, 1, 1 - t % 2, h + 1)
-
-    def attend(owner, group, halves):
+
+        @pl.when((t <= 4) | (t == 6))
+        def _():
+            pass_left(t, jnp.minimum(t + 2, TILES - 1)).start()
+
+    def arrange(t):
+        end = t == TILES - 1
+        group = 1 - lax.rem(t, 2)
+        h = t - group
+        prepare(t, 0, group, h)
+        prepare(t, 1, jnp.where(end, 1, group), jnp.where(end, h, h + 1))
+
+    def attend(owner, group, start, number):
+        halves = [start + k for k in range(number)]
         row = owner_row(group)
         every = owner > row
-        visible = [origins[h] < z for h in halves]
+        visible = [origin_of(h) < z for h in halves]
         some = visible[0]
         for v in visible[1:]:
             some = some | v
@@ -276,7 +283,7 @@
                 twice = jnp.concatenate([new_peak, new_peak], 1)
                 weights = jnp.concatenate([jnp.exp2(p - twice).astype(BF16) for p in scores[i]], 1)
                 summed = jnp.dot(
-                    weights, vv[group, pl.ds(halves[0] * HALF, len(halves) * HALF)], preferred_element_type=F32
+                    weights, vv[group, pl.ds(start * HALF, number * HALF)], preferred_element_type=F32
                 )
                 scale = jnp.exp2(old_peak - new_peak)
                 acc[owner, i] = acc[owner, i] * jnp.concatenate([scale, scale], 1) + summed
@@ -343,9 +350,10 @@
     def early(w, carry):
         @pl.when(w == 0)
         def _():
+            forward(1)
             for n in range(1, NZ):
                 table_z(n).wait_recv()
-            poll(1)
+            arrange(1)
 
         @pl.when(w == 1)
         def _():
@@ -354,7 +362,8 @@
             q_send(xplus(1), 1, 3, q_left).wait_recv()
             q_send(xplus(1), 1, 5, q_left).start()
             destinations()
-            poll(2)
+            forward(2)
+            arrange(2)
 
         @pl.when(w == 2)
         def _():
@@ -363,54 +372,53 @@
             split_queries(xplus(1))
             split_queries(xplus(NX - 1))
 
-        @pl.when(w == 4)
-        def _():
-            poll(3)
+        @pl.when(w == 5)
+        def _():
+            forward(3)
+            arrange(3)
 
         @pl.when(w == 6)
         def _():
-            poll(4)
             q_send(xplus(2), 0, 4, q_right).wait_recv()
             q_send(xplus(2), 1, 5, q_left).wait_recv()
             split_queries(xplus(2))
 
         turn = lax.div(w, 2)
         n = jnp.where(turn == 2, 3, jnp.where(turn == 3, 2, turn))
-        attend(xplus(n), lax.rem(w, 2), (0, 1, 2))
+        attend(xplus(n), lax.rem(w, 2), 0, 3)
         return carry
 
     lax.fori_loop(0, 2 * NX, early, 0)
-    poll(5)
+
+    def middle(t, carry):
+        group = 1 - lax.rem(t, 2)
+
+        def one(i, inner):
+            @pl.when(i == 2)
+            def _():
+                forward(t + 1)
+                arrange(t + 1)
+
+            attend(NX - 1 - i, group, t - group, 2)
+            return inner
+
+        lax.fori_loop(0, NX, one, 0)
+        return carry
+
+    lax.fori_loop(3, TILES - 1, middle, 0)
 
     def late(i, carry):
-        @pl.when(i < NX)
-        def _():
-            def one(group, inner):
-                @pl.when((i == 0) & (group == 1))
-                def _():
-                    poll(6)
-
-                attend(NX - 1 - i, group, (3, 4, 5, 6))
-                return inner
-
-            lax.fori_loop(0, 2, one, 0)
-
-        @pl.when(i == 0)
-        def _():
-            poll(7)
-
-        @pl.when(i >= 1)
-        def _():
-            def one(group, inner):
-                attend(NX - i, group, (7,))
-                return inner
-
-            lax.fori_loop(0, 2, one, 0)
-            finish(NX - i)
-
+        owner = NX - 1 - i
+
+        def one(group, inner):
+            attend(owner, group, TILES - 1, 1)
+            return inner
+
+        lax.fori_loop(0, 2, one, 0)
+        finish(owner)
         return carry
 
-    lax.fori_loop(0, NX + 1, late, 0)
+    lax.fori_loop(0, NX, late, 0)
 
     def rows_of(row):
         return jnp.sum(jnp.where(eye, row, 0.0), axis=1, keepdims=True)
@@ -482,7 +490,7 @@
     anywhere = pl.BlockSpec(memory_space=pl.ANY)
     return pl.pallas_call(
         kernel,
-        out_shape=jax.ShapeDtypeStruct((ROWS, QROWS), BF16),
+        out_shape=pltpu.VMEM((ROWS, QROWS), BF16),
         in_specs=[anywhere] * 6 + [pl.BlockSpec(memory_space=pltpu.SMEM)],
         out_specs=pl.BlockSpec(memory_space=vmem),
         scratch_shapes=[

time: 63.1 us -> 60.6 us (0.960)
  Pallas kernels: 60.1 us -> 58.5 us
  local copies, waits for them, and re-layouts: 1.67 us -> 0.71 us
    pallas_call x1, Pallas kernels: 60.1 us -> 58.5 us  [per_device(): pl.pallas_call(kernel, out_shape=pltpu.VMEM((ROWS, QROWS), BF16), in_spec...]
    unnamed x1, local copies, waits for them, and re-layouts: 1.67 us -> 0.71 us
where the time goes in v3:
time: 60.6 us; the launch traced here: 59.9 us
  Pallas kernels  58.5 us (97%)
  local copies, waits for them, and re-layouts  0.71 us (1%)
  between operations  0.66 us (1%)
    pallas_call x1, Pallas kernels, per_device(): pl.pallas_call(kernel, out_shape=pltpu.VMEM((ROWS, QROWS), BF16), in_spec...  58.5 us

profile of v3, /device:TPU:20, one launch (start us, length us, event | category | flops | bytes accessed | tf_op | source)
XLA Modules:
  0.0 59.9 jit_solution(8163699796225444255)
XLA Ops:
  0.7 58.5 %shard_map.73 = bf16[128,1024]{1,0:T(8,128)(2,1)S(1)} custom-call(s32[4,128]{1,0:T(4,128)} %bitcast.3, s32[1,128]{1,0:T(1,128)} %bitcast.4, s32[1,128]{1,0:T(1,128)} %bitcast.5, bf16[128,1024]{1,0:T(8,128)(2,1)} %q_hbm.1, bf16[4096,128]{1,0:T(8,128)(2,1)} %k_hbm.1, bf16[4096,128]{1,0:T(8,128)(2,1)} %v_hbm.1, s32[1]{0:T(128)S(6)} %copy.10.count_ref), custom_call_target="tpu_custom_call" | custom-call | tf_op jit(solution)/shard_map/pallas_call | solution.py:491
  59.2 0.7 %copy.9 = bf16[128,1024]{1,0:T(8,128)(2,1)} copy(bf16[128,1024]{1,0:T(8,128)(2,1)S(1)} %shard_map.73) | data formatting | bytes 524288

commit v4 on v3

--- a/solution.py
+++ b/solution.py
@@ -172,19 +172,6 @@
     ]
     for copy in q_copies:
         copy.start()
-
-    swap.wait_recv()
-    for copy in own_pass(1, 2):
-        copy.start()
-
-    for n in range(1, NX):
-        table_x(n).wait_recv()
-
-    def table_z(n):
-        return remote(table.at[z], table.at[z], tz_s.at[n], tz_r.at[n], (x, zplus(n)))
-
-    for n in range(1, NZ):
-        table_z(n).start()
 
     def split_queries(owner):
         for i in range(NX):
@@ -225,6 +212,19 @@
         weights = jnp.exp2(seen_scores - jnp.concatenate([new_peak] * 4, 1)).astype(BF16)
         acc[x, i] = jnp.dot(weights, vvd[...], preferred_element_type=F32)
         peak[x, i] = new_peak
+
+    for n in range(1, NX):
+        table_x(n).wait_recv()
+
+    def table_z(n):
+        return remote(table.at[z], table.at[z], tz_s.at[n], tz_r.at[n], (x, zplus(n)))
+
+    for n in range(1, NZ):
+        table_z(n).start()
+
+    swap.wait_recv()
+    for copy in own_pass(1, 2):
+        copy.start()
 
     def owner_row(group):
         return jnp.where(group == 0, x, mirror)
@@ -351,17 +351,16 @@
         @pl.when(w == 0)
         def _():
             forward(1)
-            for n in range(1, NZ):
-                table_z(n).wait_recv()
-            arrange(1)
-
-        @pl.when(w == 1)
-        def _():
             q_send(xplus(NX - 1), 0, 0, q_right).wait_recv()
             q_send(xplus(NX - 1), 0, 4, q_right).start()
             q_send(xplus(1), 1, 3, q_left).wait_recv()
             q_send(xplus(1), 1, 5, q_left).start()
-            destinations()
+            for n in range(1, NZ):
+                table_z(n).wait_recv()
+            arrange(1)
+
+        @pl.when(w == 1)
+        def _():
             forward(2)
             arrange(2)
 
@@ -405,20 +404,20 @@
         lax.fori_loop(0, NX, one, 0)
         return carry
 
-    lax.fori_loop(3, TILES - 1, middle, 0)
+    lax.fori_loop(3, TILES - 2, middle, 0)
+    forward(TILES - 1)
+    arrange(TILES - 1)
 
     def late(i, carry):
-        owner = NX - 1 - i
-
-        def one(group, inner):
-            attend(owner, group, TILES - 1, 1)
-            return inner
-
-        lax.fori_loop(0, 2, one, 0)
+        owner = lax.rem(i + 1, NX)
+        attend(owner, 0, TILES - 1, 1)
+        attend(owner, 1, TILES - 3, 3)
         finish(owner)
         return carry
 
     lax.fori_loop(0, NX, late, 0)
+
+    destinations()
 
     def rows_of(row):
         return jnp.sum(jnp.where(eye, row, 0.0), axis=1, keepdims=True)
@@ -427,7 +426,7 @@
         zd = zplus(n)
         return remote(fin.at[owner, zd], gath.at[z, owner], a2a_s.at[owner, n], a2a_r.at[owner, n], (x, zd))
 
-    for owner in range(NX - 1, -1, -1):
+    for owner in (1, 2, 3, 0):
         sources = [s for s in range(NX) if min(s, NX - 1 - s) <= owner]
         for n in range(1, NX):
             @pl.when(takes_part(xplus(NX - n), owner))

time: 60.6 us -> 58 us (0.957); the launches traced: 59.9 us -> 57.9 us
  Pallas kernels: 58.5 us -> 56.6 us
    pallas_call x1, Pallas kernels: 58.5 us -> 56.6 us  [per_device(): pl.pallas_call(kernel, out_shape=pltpu.VMEM((ROWS, QROWS), BF16), in_spec...]
where the time goes in v4:
time: 58 us; the launch traced here: 57.9 us
  Pallas kernels  56.6 us (98%)
  local copies, waits for them, and re-layouts  0.71 us (1%)
  between operations  0.66 us (1%)
    pallas_call x1, Pallas kernels, per_device(): pl.pallas_call(kernel, out_shape=pltpu.VMEM((ROWS, QROWS), BF16), in_spec...  56.6 us

profile of v4, /device:TPU:20, one launch (start us, length us, event | category | flops | bytes accessed | tf_op | source)
XLA Modules:
  0.0 57.9 jit_solution(1717476082027029734)
XLA Ops:
  0.7 56.6 %shard_map.73 = bf16[128,1024]{1,0:T(8,128)(2,1)S(1)} custom-call(s32[4,128]{1,0:T(4,128)} %bitcast.3, s32[1,128]{1,0:T(1,128)} %bitcast.4, s32[1,128]{1,0:T(1,128)} %bitcast.5, bf16[128,1024]{1,0:T(8,128)(2,1)} %q_hbm.1, bf16[4096,128]{1,0:T(8,128)(2,1)} %k_hbm.1, bf16[4096,128]{1,0:T(8,128)(2,1)} %v_hbm.1, s32[1]{0:T(128)S(6)} %copy.10.count_ref), custom_call_target="tpu_custom_call" | custom-call | tf_op jit(solution)/shard_map/pallas_call | solution.py:490
  57.2 0.7 %copy.9 = bf16[128,1024]{1,0:T(8,128)(2,1)} copy(bf16[128,1024]{1,0:T(8,128)(2,1)S(1)} %shard_map.73) | data formatting | bytes 524288

commit v5 on v4

--- a/solution.py
+++ b/solution.py
@@ -123,10 +123,10 @@
     for copy in loads:
         copy.wait()
     spare[...] = gather(1)
+    ring[0, 0] = gather(0)
     pl.semaphore_wait(barrier, NX - 1 + NZ - 1)
     swap = remote(spare, ring.at[0, 1], swap_s, swap_r, (mirror, z))
     swap.start()
-    ring[0, 0] = gather(0)
 
     def pass_right(source, target):
         return remote(ring.at[source, 0], ring.at[target, 0], ring_s.at[target, 0], ring_r.at[target, 0], right)
@@ -335,7 +335,7 @@
     def destinations():
         for zz in range(NZ):
             for xx in range(NX):
-                slots[zz * NX + xx:zz * NX + xx + 1, :] = lax.rem(table[zz, xx], ROWS).astype(F32)
+                slots[xx * NZ + zz:xx * NZ + zz + 1, :] = lax.rem(table[zz, xx], ROWS).astype(F32)
         wide = iota((128, QROWS), 1)
         pick = jnp.where(iota((128, QROWS), 0) == c * 4 + lax.rem(wide, 4), 1.0, 0.0).astype(BF16)
         picked = jnp.dot(slots[...].astype(BF16), pick, preferred_element_type=F32)
@@ -424,7 +424,7 @@
 
     def spread(n, owner):
         zd = zplus(n)
-        return remote(fin.at[owner, zd], gath.at[z, owner], a2a_s.at[owner, n], a2a_r.at[owner, n], (x, zd))
+        return remote(fin.at[owner, zd], gath.at[owner, z], a2a_s.at[owner, n], a2a_r.at[owner, n], (x, zd))
 
     for owner in (1, 2, 3, 0):
         sources = [s for s in range(NX) if min(s, NX - 1 - s) <= owner]
@@ -448,16 +448,20 @@
         fin[owner] = (total / weight).astype(BF16).reshape(NZ, CHUNK // NZ, HD)
         for n in range(1, NZ):
             spread(n, owner).start()
-        gath[z, owner] = fin[owner, z]
-
-    for owner in range(NX - 1, -1, -1):
+        gath[owner, z] = fin[owner, z]
+
+    placed = [None] * HEADS
+    for owner in (1, 2, 3, 0):
         for n in range(1, NZ):
             spread(n, owner).wait_recv()
-    arrived = gath[...].reshape(QROWS, HD)
+        arrived = gath[owner].reshape(CHUNK, HD)
+        for h in range(HEADS):
+            share = jnp.dot(
+                ohf[h, :, owner * CHUNK:(owner + 1) * CHUNK], arrived, preferred_element_type=F32
+            )
+            placed[h] = share if placed[h] is None else placed[h] + share
     for h in range(HEADS):
-        out_ref[:, h * HD:(h + 1) * HD] = jnp.dot(
-            ohf[h], arrived, preferred_element_type=F32
-        ).astype(BF16)
+        out_ref[:, h * HD:(h + 1) * HD] = placed[h].astype(BF16)
 
     swap.wait_send()
     for copy in own_pass(0, 1) + own_pass(1, 2):
@@ -514,7 +518,7 @@
             vmem((NX, NX, CHUNK, HD), BF16),
             vmem((NX, NX, 2, 1, 128), F32),
             vmem((NX, NZ, CHUNK // NZ, HD), BF16),
-            vmem((NZ, NX, CHUNK // NZ, HD), BF16),
+            vmem((NX, NZ, CHUNK // NZ, HD), BF16),
             vmem((NZ, NX, 1, 128), I32),
             vmem((NZ * NX, 128), F32),
             vmem((HEADS, ROWS, QROWS), BF16),

time: 58 us -> 57.6 us (level)
  no operation moved by 1% of the time
where the time goes in v5:
time: 57.6 us; the launch traced here: 57.5 us
  Pallas kernels  56.2 us (98%)
  local copies, waits for them, and re-layouts  0.71 us (1%)
  between operations  0.66 us (1%)
    pallas_call x1, Pallas kernels, per_device(): pl.pallas_call(kernel, out_shape=pltpu.VMEM((ROWS, QROWS), BF16), in_spec...  56.2 us

profile of v5, /device:TPU:20, one launch (start us, length us, event | category | flops | bytes accessed | tf_op | source)
XLA Modules:
  0.0 57.5 jit_solution(18387946768421920967)
XLA Ops:
  0.7 56.2 %shard_map.73 = bf16[128,1024]{1,0:T(8,128)(2,1)S(1)} custom-call(s32[4,128]{1,0:T(4,128)} %bitcast.3, s32[1,128]{1,0:T(1,128)} %bitcast.4, s32[1,128]{1,0:T(1,128)} %bitcast.5, bf16[128,1024]{1,0:T(8,128)(2,1)} %q_hbm.1, bf16[4096,128]{1,0:T(8,128)(2,1)} %k_hbm.1, bf16[4096,128]{1,0:T(8,128)(2,1)} %v_hbm.1, s32[1]{0:T(128)S(6)} %copy.10.count_ref), custom_call_target="tpu_custom_call" | custom-call | tf_op jit(solution)/shard_map/pallas_call | solution.py:494
  56.8 0.7 %copy.9 = bf16[128,1024]{1,0:T(8,128)(2,1)} copy(bf16[128,1024]{1,0:T(8,128)(2,1)S(1)} %shard_map.73) | data formatting | bytes 524288

commit v6 on v5

--- a/solution.py
+++ b/solution.py
@@ -314,11 +314,12 @@
             alive = bottom > 0.0
             safe = jnp.where(alive, bottom, 1.0)
             part[owner, i] = (top / safe).astype(BF16)
-            logs = jnp.where(alive, peak[owner, i] + jnp.log(safe) * math.log2(math.e), LOW)
+            tops = jnp.where(alive, peak[owner, i], LOW)
             for j in range(2):
-                partl[i, owner, j] = jnp.sum(
-                    jnp.where(eye, logs[j * 128:(j + 1) * 128], 0.0), axis=0, keepdims=True
-                )
+                rows = slice(j * 128, (j + 1) * 128)
+                top_row = jnp.sum(jnp.where(eye, tops[rows], 0.0), axis=0, keepdims=True)
+                sum_row = jnp.sum(jnp.where(eye, safe[rows], 0.0), axis=0, keepdims=True)
+                partl[i, owner, j] = top_row + jnp.log(sum_row) * math.log2(math.e)
 
         @pl.when(takes_part(x, owner))
         def _():

time: 57.6 us -> 57.6 us (level)
  no operation moved by 1% of the time
where the time goes in v6:
time: 57.6 us; the launch traced here: 57.5 us
  Pallas kernels  56.1 us (97%)
  local copies, waits for them, and re-layouts  0.71 us (1%)
  between operations  0.66 us (1%)
    pallas_call x1, Pallas kernels, per_device(): pl.pallas_call(kernel, out_shape=pltpu.VMEM((ROWS, QROWS), BF16), in_spec...  56.1 us

profile of v6, /device:TPU:20, one launch (start us, length us, event | category | flops | bytes accessed | tf_op | source)
XLA Modules:
  0.0 57.5 jit_solution(13209289534838557860)
XLA Ops:
  0.7 56.1 %shard_map.73 = bf16[128,1024]{1,0:T(8,128)(2,1)S(1)} custom-call(s32[4,128]{1,0:T(4,128)} %bitcast.3, s32[1,128]{1,0:T(1,128)} %bitcast.4, s32[1,128]{1,0:T(1,128)} %bitcast.5, bf16[128,1024]{1,0:T(8,128)(2,1)} %q_hbm.1, bf16[4096,128]{1,0:T(8,128)(2,1)} %k_hbm.1, bf16[4096,128]{1,0:T(8,128)(2,1)} %v_hbm.1, s32[1]{0:T(128)S(6)} %copy.10.count_ref), custom_call_target="tpu_custom_call" | custom-call | tf_op jit(solution)/shard_map/pallas_call | solution.py:495
  56.8 0.7 %copy.9 = bf16[128,1024]{1,0:T(8,128)(2,1)} copy(bf16[128,1024]{1,0:T(8,128)(2,1)S(1)} %shard_map.73) | data formatting | bytes 524288
